TPU v7x, 256 devices: a whole 4x4x8 slice. The times are simulated.
256 devices in a mesh: row: 32 (over x, z_hi, core), col: 8 (over z_lo, y).
Axes of the slice: x: 4, y: 4, z: 8 (z_hi: 4, z_lo: 2; z = z_hi * 2 + z_lo), core: 2. Of those that a mesh axis runs over, the one named last changes fastest.
Arguments:
- sim: bfloat16 [7168, 7168], P('row', 'col'), may hold values from 0 to 2304, as said below
- live: int32 [56, 56], P(None, 'col'), may hold values from 0 to 1, as said below
Outputs:
- flow: float32 [7168, 7168], P('row', 'col')
Inputs may be any that keep to these rules, and one draw needn't show every extreme that they name: sim is symmetric and nonnegative, with a positive diagonal. live is symmetric, with ones on its diagonal.
All inputs are finite; a program needn't handle non-finite values.
Results may differ from a plain program's by a relative error of at most 0.00067.
Values may be sent and summed in bfloat16 or wider, within the bound.
A program may use at most 128 MiB of HBM per device.

v0:
```python
import jax
import jax.numpy as jnp
from jax import lax
from jax.sharding import PartitionSpec as P


def tile_mask(sim, live):
    rows_here, cols_here = sim.shape
    tile_count, col_tiles = live.shape
    tile_width = cols_here // col_tiles
    first_row = lax.axis_index("row") * rows_here
    owner_tile = (first_row + jnp.arange(rows_here, dtype=jnp.int32)) // tile_width
    picker = (owner_tile[:, None] == jnp.arange(tile_count, dtype=jnp.int32)[None, :]).astype(
        jnp.float32
    )
    marked = jnp.dot(picker, live.astype(jnp.float32), preferred_element_type=jnp.float32)
    spread = jnp.broadcast_to(marked[:, :, None], (rows_here, col_tiles, tile_width)).reshape(
        rows_here, cols_here
    )
    return sim * spread.astype(jnp.bfloat16)


def per_device(sim, live):
    rows_here, cols_here = sim.shape
    linked = tile_mask(sim, live)
    row_panel = lax.all_gather(linked, "col", axis=1, tiled=True)
    degree = lax.psum(jnp.sum(linked, axis=1, dtype=jnp.float32), "col")
    weighted = (linked.astype(jnp.float32) / degree[:, None]).astype(jnp.bfloat16)
    expanded = lax.psum_scatter(
        lax.dot_general(
            row_panel, weighted, (((0,), (0,)), ((), ())), preferred_element_type=jnp.float32
        ),
        "row",
        scatter_dimension=0,
        tiled=True,
    )
    inflated = expanded * expanded
    total = lax.psum(jnp.sum(inflated, axis=0), "row")
    nodes_all = rows_here * lax.axis_size("row")
    return nodes_all * inflated / total[None, :]


def solution(mesh):
    in_specs = (P("row", "col"), P(None, "col"))
    out_specs = P("row", "col")
    return jax.shard_map(
        per_device, mesh=mesh, in_specs=in_specs, out_specs=out_specs, check_vma=False
    )
```

profile of v0, /device:TPU:32, one launch (start us, length us, event | category | flops | bytes accessed | tf_op | source)
XLA Modules:
  0.0 372.4 jit_solution(8984071443376596182)
XLA Ops:
  6.5 0.0 all-gather.2.cloned.1.call-start
  6.5 0.9 convolution_convert_fusion
  7.5 0.2 copy.4
  7.6 0.3 broadcast_in_dim.2
  8.0 1.9 convert_reduce_fusion
  9.8 0.0 all-gather.2.cloned.1.call-update
  9.9 0.0 reduce-scatter.2.cloned.1.call-start
  9.9 18.5 %psum.14 = f32[224]{0:T(256)S(1)} all-reduce(f32[224]{0:T(256)S(1)} %get-tuple-element.5), channel_id=1, replica_groups=mesh['row'=32,'col'=8] {'col'}, use_global_device_ids=true, to_apply=%region_1.2 | all-reduce | flops 224 | bytes 1792 | tf_op jit(solution)/shard_map/psum | solution.py:27
  28.4 30.4 %all-gather.2.cloned.1.call-done = bf16[224,7168]{1,0:T(8,128)(2,1)} async-done(((bf16[224,896]{1,0:T(8,128)(2,1)}), bf16[224,7168]{1,0:T(8,128)(2,1)}) %all-gather.2.cloned.1.call-update) | async-done | bytes 3211280 | tf_op jit(solution)/shard_map/all_gather | solution.py:26
  58.8 14.6 %fusion.1 = f32[7168,896]{1,0:T(8,128)} fusion(bf16[224,7168]{1,0:T(8,128)(2,1)} %all-gather.2.cloned.1.call-done, bf16[224,896]{1,0:T(8,128)(2,1)} %get-tuple-element.6, f32[224]{0:T(256)S(1)} %psum.14), kind=kOutput, calls=%fused_computation.6 | convolution fusion | flops 2877894656 | bytes 29303680 | tf_op jit(solution)/shard_map/dot_general | solution.py:30
  73.4 0.0 reduce-scatter.2.cloned.1.call-update
  73.4 214.2 %reduce-scatter.2.cloned.1.call-done = f32[224,896]{1,0:T(8,128)} async-done(((f32[7168,896]{1,0:T(8,128)}), f32[224,896]{1,0:T(8,128)}) %reduce-scatter.2.cloned.1.call-update) | async-done | bytes 802832 | tf_op jit(solution)/shard_map/reduce_scatter | solution.py:29
  287.6 1.2 multiply_reduce_fusion
  288.8 74.6 %psum.15 = f32[896]{0:T(1024)S(1)} all-reduce(f32[896]{0:T(1024)S(1)} %multiply_reduce_fusion), channel_id=1, replica_groups=mesh['row'=32,'col'=8] {'row'}, use_global_device_ids=true, to_apply=%region_4.5 | all-reduce | flops 896 | bytes 7168 | tf_op jit(solution)/shard_map/psum | solution.py:38
  363.4 2.1 multiply_divide_fusion
  (1 shorter events, 0.0 us)
Async XLA Ops:
  6.5 52.3 %all-gather.2.cloned.1.call-start = ((), (), s32[]{:S(2)}) async-start(), calls=%async_computation.1 | async-start | bytes 3612672 | tf_op jit(solution)/shard_map/all_gather | solution.py:26
  9.9 277.8 %reduce-scatter.2.cloned.1.call-start = ((), (), s32[]{:S(2)}) async-start(), calls=%async_computation.2 | async-start | bytes 26492928 | tf_op jit(solution)/shard_map/reduce_scatter | solution.py:29
Sparse Core Ops, SparseCore 0:
  10.0 48.8 all-gather.1
  73.5 214.0 reduce-scatter.1
where the time goes:
time: 375 us; the launch traced here: 372 us
  waiting for transfers between devices  245 us (65%)
  blocking collectives  93.1 us (25%)
  matrix products  15.5 us (4%)
  between operations  13.4 us (4%)
  other arithmetic  5.2 us (1%)
    reduce_scatter x1, waiting for transfers between devices, per_device(): lax.psum_scatter(lax.dot_general(row_panel, weighted, (((0,), (0,)), ((),...  214 us
    psum x1, blocking collectives, per_device(): total = lax.psum(jnp.sum(inflated, axis=0), 'row')  74.6 us
    all_gather x1, waiting for transfers between devices, per_device(): row_panel = lax.all_gather(linked, 'col', axis=1, tiled=True)  30.4 us
    psum x1, blocking collectives, per_device(): degree = lax.psum(jnp.sum(linked, axis=1, dtype=jnp.float32), 'col')  18.5 us
    dot_general x1, matrix products, per_device(): lax.dot_general(row_panel, weighted, (((0,), (0,)), ((), ())), preferred_...  14.6 us
  transfers between devices with their start and end apart: 2, of which 2 were waited for; matrix products, arithmetic and copies ran while one was open for 0% of the time, Pallas kernels for 0%

commit v1 on v0

v1 whole, which is shorter than its diff:
```python
import jax
import jax.numpy as jnp
from jax import lax
from jax.experimental import pallas as pl
from jax.experimental.pallas import tpu as pltpu
from jax.sharding import PartitionSpec as P

MESH = pl.DeviceIdType.MESH
TILE = 128
STRIP = 32
ROWS = 224
COLS = 896
ROW_DEVICES = 32
COL_DEVICES = 8
NODES = 7168
HALF = 96
TOP, BOTTOM, EDGE, EDGE_TOP, EDGE_BOTTOM = 0, 1, 2, 3, 4
PIECES = {
    TOP: (0, HALF),
    BOTTOM: (HALF, HALF),
    EDGE: (2 * HALF, ROWS - 2 * HALF),
    EDGE_TOP: (2 * HALF, (ROWS - 2 * HALF) // 2),
    EDGE_BOTTOM: (2 * HALF + (ROWS - 2 * HALF) // 2, (ROWS - 2 * HALF) // 2),
}
PANEL_HALF = ROWS // 2
SENDS = 112


def kernel(
    sim_ref,
    live_ref,
    out_ref,
    panel,
    weighted,
    expanded,
    degree_own,
    degree_pair,
    degree_sum,
    degree_in,
    total_own,
    total_core,
    total_x,
    total_z,
    send_sem,
    recv_w,
    recv_core,
    recv_a,
    recv_small,
):
    row, col = lax.axis_index("row"), lax.axis_index("col")
    x, zh, core = row // 8, (row // 2) % 4, row % 2
    zl, y = col // 4, col % 4

    def to_x(d):
        return ((x + d + 4) % 4 * 4 + zh) * 2 + core, col

    def to_z(d):
        return (x * 4 + (zh + d + 4) % 4) * 2 + core, col

    def to_y(d):
        return row, zl * 4 + (y + d + 4) % 4

    to_pair = (row, (1 - zl) * 4 + y)
    to_core = (row + 1 - 2 * core, col)

    barrier = pltpu.get_barrier_semaphore()
    partners = [to(d) for to in (to_x, to_y, to_z) for d in (1, 2, 3)] + [to_pair, to_core]
    for device in partners:
        pl.semaphore_signal(barrier, 1, device_id=device, device_id_type=MESH)

    for s in range(ROWS // STRIP):
        tile_row = (row * (ROWS // STRIP) + s) // (TILE // STRIP)
        for t in range(COLS // TILE):
            mark = live_ref[tile_row, t].astype(jnp.float32)
            strip = sim_ref[s * STRIP : (s + 1) * STRIP, t * TILE : (t + 1) * TILE]
            panel[col, s * STRIP : (s + 1) * STRIP, t * TILE : (t + 1) * TILE] = (
                strip.astype(jnp.float32) * mark
            ).astype(jnp.bfloat16)
    adj = panel[col]
    ones = jnp.ones((8, COLS), jnp.bfloat16)
    sums = lax.dot_general(
        ones, adj, (((1,), (1,)), ((), ())), preferred_element_type=jnp.float32
    )
    degree_own[...] = jnp.zeros_like(degree_own)
    degree_own[:, :ROWS] = sums

    pl.semaphore_wait(barrier, len(partners))

    sends = []

    def send(src, dst, recv, device):
        copy = pltpu.make_async_remote_copy(
            src, dst, send_sem.at[len(sends)], recv, device_id=device, device_id_type=MESH
        )
        copy.start()
        sends.append(copy)

    def arrived(ref, recv):
        pltpu.make_async_remote_copy(
            ref, ref, send_sem.at[0], recv, device_id=to_core, device_id_type=MESH
        ).wait_recv()

    def a_ref(pair, dy, half):
        slot = (zl if pair == 0 else 1 - zl) * 4 + (y + dy + 4) % 4
        return panel.at[slot, pl.ds(half * PANEL_HALF, PANEL_HALF)]

    def a_send_pair(half):
        ref = a_ref(0, 0, half)
        send(ref, ref, recv_a.at[1, 0, half], to_pair)

    def a_send_y(pair, dy, half, step):
        ref = a_ref(pair, dy, half)
        send(ref, ref, recv_a.at[pair, (dy - step) % 4, half], to_y(step))

    def a_wait(pair, dy, half):
        arrived(a_ref(pair, dy, half), recv_a.at[pair, dy % 4, half])

    def w_row(dx, dz, which):
        return (((x + dx + 4) % 4) * 4 + (zh + dz + 4) % 4) * 2 + which

    def w_ref(dx, dz, piece):
        start, size = PIECES[piece]
        first = pl.multiple_of(w_row(dx, dz, core) * ROWS + start, 16)
        return weighted.at[pl.ds(first, size)]

    def w_send(dx, dz, piece, axis, step):
        ref = w_ref(dx, dz, piece)
        nx, nz = (dx - step, dz) if axis == 0 else (dx, dz - step)
        send(
            ref,
            ref,
            recv_w.at[nx % 4, nz % 4, piece],
            to_x(step) if axis == 0 else to_z(step),
        )

    def w_wait(dx, dz, piece):
        arrived(w_ref(dx, dz, piece), recv_w.at[dx % 4, dz % 4, piece])

    def w_block(dx, dz, which):
        return weighted.at[pl.ds(pl.multiple_of(w_row(dx, dz, which) * ROWS, 16), ROWS)]

    def share(dx, dz):
        ref = w_block(dx, dz, core)
        send(ref, ref, recv_core.at[dx % 4, dz % 4], to_core)

    def shared(dx, dz):
        arrived(w_block(dx, dz, 1 - core), recv_core.at[dx % 4, dz % 4])

    send(degree_own, degree_pair, recv_small.at[0], to_pair)
    for half in (0, 1):
        a_send_pair(half)
    for half in (0, 1):
        a_send_y(0, 0, half, 1)
        a_send_y(0, 0, 1 - half, -1)
    arrived(degree_pair, recv_small.at[0])
    degree_sum[...] = degree_own[...] + degree_pair[...]
    for d in (1, 3, 2):
        send(degree_sum, degree_in.at[4 - d], recv_small.at[4 - d], to_y(d))
    degree = degree_sum[...]
    for d in (1, 3, 2):
        arrived(degree_in.at[d], recv_small.at[d])
        degree += degree_in[d]
    degree_column = jnp.transpose(degree)[:ROWS, 0:1]
    own = pl.multiple_of(row * ROWS, 16)
    weighted[pl.ds(own, ROWS), :] = (adj.astype(jnp.float32) / degree_column).astype(
        jnp.bfloat16
    )

    w_send(0, 0, TOP, 1, 1)
    w_send(0, 0, BOTTOM, 1, -1)
    w_send(0, 0, TOP, 0, 1)
    w_send(0, 0, BOTTOM, 0, -1)
    w_send(0, 0, EDGE, 0, 1)
    w_send(0, 0, EDGE, 0, -1)
    w_send(0, 0, BOTTOM, 1, 1)
    w_send(0, 0, TOP, 1, -1)
    w_send(0, 0, BOTTOM, 0, 1)
    w_send(0, 0, TOP, 0, -1)
    w_send(0, 0, EDGE, 1, 1)
    w_send(0, 0, EDGE, 1, -1)
    share(0, 0)

    def along_x(dz, piece):
        w_send(0, dz, piece, 0, 1)
        w_send(0, dz, piece, 0, -1)

    def along_z(dx):
        w_send(dx, 0, EDGE, 1, 1)
        w_send(dx, 0, EDGE, 1, -1)

    def pass_x(dz):
        w_wait(-1, dz, TOP)
        w_send(-1, dz, TOP, 0, 1)
        w_wait(1, dz, BOTTOM)
        w_send(1, dz, BOTTOM, 0, -1)

    def rest_x(dz):
        w_wait(-1, dz, BOTTOM)
        w_wait(1, dz, TOP)

    def last_x(dz):
        w_wait(2, dz, TOP)
        w_wait(2, dz, BOTTOM)

    def pass_z(dx):
        w_wait(dx, -1, EDGE)
        w_send(dx, -1, EDGE_TOP, 1, 1)
        w_wait(dx, 1, EDGE)
        w_send(dx, 1, EDGE_BOTTOM, 1, -1)

    def last_z(dx):
        w_wait(dx, 2, EDGE_TOP)
        w_wait(dx, 2, EDGE_BOTTOM)

    def multiply(dx, first):
        xx = (x + dx) % 4

        for start in range(0, COLS, 256):
            size = min(256, COLS - start)
            acc = None
            for half in (0, 1):
                depth = pl.multiple_of((xx * 2 + half) * COLS, 16)
                part = jnp.dot(
                    panel[xx * 2 + half],
                    weighted[pl.ds(depth, COLS), start : start + size],
                    preferred_element_type=jnp.float32,
                )
                acc = part if acc is None else acc + part
            if first:
                expanded[:, start : start + size] = acc
            else:
                expanded[:, start : start + size] += acc

    w_wait(0, -1, TOP)
    w_send(0, -1, TOP, 1, 1)
    along_x(-1, TOP)
    w_wait(0, 1, BOTTOM)
    w_send(0, 1, BOTTOM, 1, -1)
    along_x(1, BOTTOM)
    pass_x(0)
    w_wait(-1, 0, EDGE)
    w_send(-1, 0, EDGE_TOP, 0, 1)
    along_z(-1)
    w_wait(1, 0, EDGE)
    w_send(1, 0, EDGE_BOTTOM, 0, -1)
    along_z(1)
    for half in (0, 1):
        a_wait(1, 0, half)
        a_send_y(1, 0, half, 1)
        a_send_y(1, 0, half, -1)
    a_wait(0, -1, 0)
    a_send_y(0, -1, 0, 1)
    a_wait(0, 1, 1)
    a_send_y(0, 1, 1, -1)
    w_wait(0, -1, BOTTOM)
    along_x(-1, BOTTOM)
    w_wait(0, 1, TOP)
    along_x(1, TOP)
    rest_x(0)
    share(-1, 0)
    share(1, 0)
    w_wait(2, 0, EDGE_TOP)
    w_wait(2, 0, EDGE_BOTTOM)
    along_z(2)
    last_x(0)
    share(2, 0)
    pass_z(0)
    share(0, -1)
    share(0, 1)
    w_wait(0, 2, TOP)
    along_x(2, TOP)
    w_wait(0, 2, BOTTOM)
    along_x(2, BOTTOM)
    pass_x(-1)
    pass_z(-1)
    pass_x(1)
    pass_z(1)
    last_z(0)
    share(0, 2)
    a_wait(1, -1, 0)
    a_send_y(1, -1, 0, 1)
    a_wait(1, 1, 1)
    a_send_y(1, 1, 1, -1)
    rest_x(-1)
    share(-1, -1)
    share(1, -1)
    rest_x(1)
    share(-1, 1)
    share(1, 1)
    pass_z(2)
    last_x(-1)
    share(2, -1)
    last_x(1)
    share(2, 1)
    pass_x(2)
    for pair in (0, 1):
        for dy, half in ((-1, 1), (1, 0), (2, 0), (2, 1)):
            a_wait(pair, dy, half)
    for dz in (0, -1, 1, 2):
        shared(0, dz)
    multiply(0, True)
    rest_x(2)
    last_z(-1)
    share(-1, 2)
    last_z(1)
    share(1, 2)
    last_z(2)
    last_x(2)
    share(2, 2)
    for dx in (-1, 1, 2):
        for dz in (0, -1, 1, 2):
            shared(dx, dz)
        multiply(dx, False)

    inflated = expanded[...] * expanded[...]
    part = jnp.sum(inflated.reshape(ROWS // 8, 8, COLS), axis=0)
    total_own[0] = part
    send(total_own.at[0], total_core, recv_small.at[4], to_core)
    arrived(total_core, recv_small.at[4])
    part += total_core[...]
    total_own[1] = part
    for d in (1, 3, 2):
        send(total_own.at[1], total_x.at[4 - d], recv_small.at[4 + 4 - d], to_x(d))
    for d in (1, 3, 2):
        arrived(total_x.at[d], recv_small.at[4 + d])
        part += total_x[d]
    total_own[2] = part
    for d in (1, 3, 2):
        send(total_own.at[2], total_z.at[4 - d], recv_small.at[8 + 4 - d], to_z(d))
    for d in (1, 3, 2):
        arrived(total_z.at[d], recv_small.at[8 + d])
        part += total_z[d]
    total = jnp.sum(part, axis=0, keepdims=True)
    out_ref[...] = NODES * inflated / total
    for copy in sends:
        copy.wait_send()


def per_device(sim, live):
    small = pltpu.VMEM((8, 256), jnp.float32)
    wide = (8, COLS)
    return pl.pallas_call(
        kernel,
        out_shape=jax.ShapeDtypeStruct((ROWS, COLS), jnp.float32),
        in_specs=[
            pl.BlockSpec(memory_space=pltpu.VMEM),
            pl.BlockSpec(memory_space=pltpu.SMEM),
        ],
        out_specs=pl.BlockSpec(memory_space=pltpu.VMEM),
        scratch_shapes=[
            pltpu.VMEM((COL_DEVICES, ROWS, COLS), jnp.bfloat16),
            pltpu.VMEM((NODES, COLS), jnp.bfloat16),
            pltpu.VMEM((ROWS, COLS), jnp.float32),
            small,
            small,
            small,
            pltpu.VMEM((4, 8, 256), jnp.float32),
            pltpu.VMEM((3, *wide), jnp.float32),
            pltpu.VMEM(wide, jnp.float32),
            pltpu.VMEM((4, *wide), jnp.float32),
            pltpu.VMEM((4, *wide), jnp.float32),
            pltpu.SemaphoreType.DMA((SENDS,)),
            pltpu.SemaphoreType.DMA((4, 4, 5)),
            pltpu.SemaphoreType.DMA((4, 4)),
            pltpu.SemaphoreType.DMA((2, 4, 2)),
            pltpu.SemaphoreType.DMA((12,)),
        ],
        compiler_params=pltpu.CompilerParams(
            collective_id=0, has_side_effects=True, vmem_limit_bytes=56 * 2**20
        ),
        name="expand_inflate",
    )(sim, live)


def solution(mesh):
    return jax.shard_map(
        per_device,
        mesh=mesh,
        in_specs=(P("row", "col"), P(None, "col")),
        out_specs=P("row", "col"),
        check_vma=False,
    )
```

time: 375 us -> 94.5 us (0.25)
  waiting for transfers between devices: 245 us -> 0 us
  blocking collectives: 93.1 us -> 0 us
  Pallas kernels: 0 us -> 90.8 us
  matrix products: 15.5 us -> 0 us
  between operations: 13.4 us -> 0.01 us
  other arithmetic: 5.2 us -> 0 us
    reduce_scatter x1 -> x0, waiting for transfers between devices: 214 us -> none  [per_device(): lax.psum_scatter(lax.dot_general(row_panel, weighted, (((0,), (0,)), ((),...]
    psum x2 -> x0, blocking collectives: 93.1 us -> none  [the longest x1 74.6 us: per_device(): total = lax.psum(jnp.sum(inflated, axis=0), 'row')]
    pallas_call x0 -> x1, Pallas kernels: none -> 90.8 us  [per_device(): pl.pallas_call(kernel, out_shape=jax.ShapeDtypeStruct((ROWS, COLS), jnp.f...]
    all_gather x1 -> x0, waiting for transfers between devices: 30.4 us -> none  [per_device(): row_panel = lax.all_gather(linked, 'col', axis=1, tiled=True)]
    dot_general x2 -> x0, matrix products: 15.5 us -> none  [the longest x1 14.6 us: per_device(): lax.dot_general(row_panel, weighted, (((0,), (0,)), ((), ())), preferred_...]
  transfers between devices with their start and end apart: 2 -> 0, of which waited for: 2 -> 0; matrix products, arithmetic and copies ran while one was open for 0% -> 0% of each run, Pallas kernels for 0% -> 0%
where the time goes in v1:
time: 94.5 us; the launch traced here: 94.3 us
  Pallas kernels  90.8 us (96%)
  local copies, waits for them, and re-layouts  3.46 us (4%)
    pallas_call x1, Pallas kernels, per_device(): pl.pallas_call(kernel, out_shape=jax.ShapeDtypeStruct((ROWS, COLS), jnp.f...  90.8 us
    unnamed x2, local copies, waits for them, and re-layouts  3.46 us

profile of v1, /device:TPU:32, one launch (start us, length us, event | category | flops | bytes accessed | tf_op | source)
XLA Modules:
  0.0 94.3 jit_solution(15539414079192558698)
XLA Ops:
  0.0 1.4 %copy.3.live_ref = s32[56,7]{1,0:T(8,128)} copy(s32[56,7]{0,1:T(8,128)} %param.3) | data formatting | bytes 3136 | tf_op args[1]
  1.4 90.8 %expand_inflate.1 = f32[224,896]{1,0:T(8,128)} custom-call(bf16[224,896]{1,0:T(8,128)(2,1)} %sim_ref.1, s32[56,7]{1,0:T(8,128)} %copy.3.live_ref), custom_call_target="tpu_custom_call" | custom-call | tf_op jit(solution)/shard_map/expand_inflate/pallas_call | solution.py:342
  92.2 2.1 %copy.5 = f32[224,896]{1,0:T(8,128)} copy(f32[224,896]{1,0:T(8,128)} %expand_inflate.1) | data formatting | bytes 1605632

commit v2 on v1

--- a/solution.py
+++ b/solution.py
@@ -1,5 +1,8 @@
+import functools
+
 import jax
 import jax.numpy as jnp
+import numpy as np
 from jax import lax
 from jax.experimental import pallas as pl
 from jax.experimental.pallas import tpu as pltpu
@@ -13,40 +16,55 @@
 ROW_DEVICES = 32
 COL_DEVICES = 8
 NODES = 7168
-HALF = 96
 TOP, BOTTOM, EDGE, EDGE_TOP, EDGE_BOTTOM = 0, 1, 2, 3, 4
-PIECES = {
-    TOP: (0, HALF),
-    BOTTOM: (HALF, HALF),
-    EDGE: (2 * HALF, ROWS - 2 * HALF),
-    EDGE_TOP: (2 * HALF, (ROWS - 2 * HALF) // 2),
-    EDGE_BOTTOM: (2 * HALF + (ROWS - 2 * HALF) // 2, (ROWS - 2 * HALF) // 2),
-}
+
+
+def parts_of(half, edge):
+    return {
+        TOP: (0, half),
+        BOTTOM: (half, half),
+        EDGE: (2 * half, 2 * edge),
+        EDGE_TOP: (2 * half, edge),
+        EDGE_BOTTOM: (2 * half + edge, edge),
+    }
+
+
+ROW_PARTS = parts_of(96, 16)
+SLOTS = 22
+SLOT_PARTS = parts_of(9, 2)
+STRIPS = ROWS // STRIP
+SHARE = 2 * STRIPS
+SPOTS = 4 * SHARE
 PANEL_HALF = ROWS // 2
 SENDS = 112
 
 
-def kernel(
-    sim_ref,
-    live_ref,
-    out_ref,
-    panel,
-    weighted,
-    expanded,
-    degree_own,
-    degree_pair,
-    degree_sum,
-    degree_in,
-    total_own,
-    total_core,
-    total_x,
-    total_z,
-    send_sem,
-    recv_w,
-    recv_core,
-    recv_a,
-    recv_small,
-):
+def place_tables():
+    place = np.arange(TILE)
+    source, s, u = place // SHARE, place % SHARE // 2, place % 2
+    used = place < SPOTS
+    tile_rows = np.zeros((8, NODES // TILE, TILE))
+    for zh in range(4):
+        for core in range(2):
+            block = (source * 4 + zh) * 2 + core
+            tile = (block * STRIPS + s) // (TILE // STRIP)
+            tile_rows[zh * 2 + core] = used & (np.arange(NODES // TILE)[:, None] == tile)
+    tile_cols = np.zeros((4, 8, TILE))
+    for q in range(4):
+        tile_cols[q] = used & (np.arange(8)[:, None] == (q - s) % 4 + 4 * u)
+    before = place[:, None] < place[None, :]
+    flat = [m.reshape(-1, TILE) for m in (tile_rows, tile_cols, before)]
+    return np.concatenate(flat).astype(jnp.bfloat16)
+
+
+def kernel(sparse, *refs):
+    if sparse:
+        (sim_ref, live_ref, marks_ref, tables_ref, out_ref, flag_ref, *refs) = refs
+        (packed, out_share, in_share, stage, mark, order, table, table_smem, take, take_smem, copy_sem, *refs) = refs
+    else:
+        sim_ref, live_ref, out_ref, *refs = refs
+    (panel, weighted, expanded, degree_own, degree_pair, degree_sum, degree_in, total_own, total_core, total_x, total_z, *refs) = refs
+    send_sem, recv_w, recv_core, recv_a, recv_small, recv_share = refs
     row, col = lax.axis_index("row"), lax.axis_index("col")
     x, zh, core = row // 8, (row // 2) % 4, row % 2
     zl, y = col // 4, col % 4
@@ -71,10 +89,10 @@
     for s in range(ROWS // STRIP):
         tile_row = (row * (ROWS // STRIP) + s) // (TILE // STRIP)
         for t in range(COLS // TILE):
-            mark = live_ref[tile_row, t].astype(jnp.float32)
+            kept = live_ref[t, tile_row].astype(jnp.float32)
             strip = sim_ref[s * STRIP : (s + 1) * STRIP, t * TILE : (t + 1) * TILE]
             panel[col, s * STRIP : (s + 1) * STRIP, t * TILE : (t + 1) * TILE] = (
-                strip.astype(jnp.float32) * mark
+                strip.astype(jnp.float32) * kept
             ).astype(jnp.bfloat16)
     adj = panel[col]
     ones = jnp.ones((8, COLS), jnp.bfloat16)
@@ -84,6 +102,43 @@
     degree_own[...] = jnp.zeros_like(degree_own)
     degree_own[:, :ROWS] = sums
 
+    if sparse:
+        marks = marks_ref[...].astype(jnp.float32).astype(jnp.bfloat16)
+        tiles = NODES // TILE
+        for zc in range(8):
+            picked = jnp.dot(
+                marks,
+                tables_ref[zc * tiles : (zc + 1) * tiles, :],
+                preferred_element_type=jnp.float32,
+            )
+            for q in range(4):
+                first = 8 * tiles + q * 8
+                columns = tables_ref[first : first + 8, :].astype(jnp.float32)[: COLS // TILE]
+                mark[q * 8 + zc : q * 8 + zc + 1, :] = jnp.sum(
+                    picked * columns, axis=0, keepdims=True
+                )
+        live = mark[...]
+        before = jnp.dot(
+            live.astype(jnp.bfloat16),
+            tables_ref[8 * tiles + 32 :, :],
+            preferred_element_type=jnp.float32,
+        )
+        order[...] = before + live
+        most = jnp.max(jnp.max(before + live, axis=1, keepdims=True), axis=0, keepdims=True)
+        degree_own[:, ROWS:] = jnp.broadcast_to(most, (8, 256 - ROWS))
+        table[...] = jnp.where((live > 0) & (before < SLOTS), before, SLOTS).astype(jnp.int32)
+        slot = lax.broadcasted_iota(jnp.int32, (32, TILE), 0).astype(jnp.float32)
+        spot = lax.broadcasted_iota(jnp.int32, (32, TILE), 1)
+        passed = jnp.where((order[pl.ds(row, 1), :] <= slot) & (spot < SPOTS), 1.0, 0.0)
+        index = jnp.minimum(jnp.sum(passed, axis=1, keepdims=True), SPOTS - 1.0)
+        take[...] = jnp.broadcast_to(index, (32, TILE)).astype(jnp.int32)
+        table_copy = pltpu.make_async_copy(table, table_smem, copy_sem.at[0])
+        take_copy = pltpu.make_async_copy(take, take_smem, copy_sem.at[1])
+        table_copy.start()
+        take_copy.start()
+        out_share[...] = jnp.zeros_like(out_share)
+        stage[SLOTS] = jnp.zeros((STRIP, TILE), jnp.bfloat16)
+
     pl.semaphore_wait(barrier, len(partners))
 
     sends = []
@@ -119,7 +174,10 @@
         return (((x + dx + 4) % 4) * 4 + (zh + dz + 4) % 4) * 2 + which
 
     def w_ref(dx, dz, piece):
-        start, size = PIECES[piece]
+        if sparse:
+            start, size = SLOT_PARTS[piece]
+            return packed.at[w_row(dx, dz, core), pl.ds(start, size)]
+        start, size = ROW_PARTS[piece]
         first = pl.multiple_of(w_row(dx, dz, core) * ROWS + start, 16)
         return weighted.at[pl.ds(first, size)]
 
@@ -137,6 +195,8 @@
         arrived(w_ref(dx, dz, piece), recv_w.at[dx % 4, dz % 4, piece])
 
     def w_block(dx, dz, which):
+        if sparse:
+            return packed.at[w_row(dx, dz, which)]
         return weighted.at[pl.ds(pl.multiple_of(w_row(dx, dz, which) * ROWS, 16), ROWS)]
 
     def share(dx, dz):
@@ -153,18 +213,42 @@
         a_send_y(0, 0, half, 1)
         a_send_y(0, 0, 1 - half, -1)
     arrived(degree_pair, recv_small.at[0])
-    degree_sum[...] = degree_own[...] + degree_pair[...]
+    lane = lax.broadcasted_iota(jnp.int32, (8, 256), 1)
+
+    def join(a, b):
+        return jnp.where(lane < ROWS, a + b, jnp.maximum(a, b))
+
+    degree_sum[...] = join(degree_own[...], degree_pair[...])
     for d in (1, 3, 2):
         send(degree_sum, degree_in.at[4 - d], recv_small.at[4 - d], to_y(d))
     degree = degree_sum[...]
     for d in (1, 3, 2):
         arrived(degree_in.at[d], recv_small.at[d])
-        degree += degree_in[d]
+        degree = join(degree, degree_in[d])
     degree_column = jnp.transpose(degree)[:ROWS, 0:1]
-    own = pl.multiple_of(row * ROWS, 16)
-    weighted[pl.ds(own, ROWS), :] = (adj.astype(jnp.float32) / degree_column).astype(
-        jnp.bfloat16
-    )
+    scaled = (adj.astype(jnp.float32) / degree_column).astype(jnp.bfloat16)
+    if sparse:
+        flag_ref[...] = degree[:, TILE:]
+        for q in range(4):
+            for s in range(STRIPS):
+                for u in (0, 1):
+                    t = (q - s) % 4 + 4 * u
+                    if t < COLS // TILE:
+                        out_share[q, s * 2 + u] = scaled[
+                            s * STRIP : (s + 1) * STRIP, t * TILE : (t + 1) * TILE
+                        ]
+        for d in (2, 1, 3):
+            there = (x + d) % 4
+            send(out_share.at[there], in_share.at[pl.ds(x * SHARE, SHARE)], recv_share.at[4 - d], to_x(d))
+        in_share[pl.ds(x * SHARE, SHARE)] = out_share[x]
+        table_copy.wait()
+        take_copy.wait()
+        for d in (1, 3, 2):
+            arrived(in_share.at[pl.ds((x + d) % 4 * SHARE, SHARE)], recv_share.at[d])
+        for k in range(SLOTS):
+            packed[row, k] = in_share[jnp.clip(take_smem[k, 0], 0, SPOTS - 1)]
+    else:
+        weighted[pl.ds(pl.multiple_of(row * ROWS, 16), ROWS), :] = scaled
 
     w_send(0, 0, TOP, 1, 1)
     w_send(0, 0, BOTTOM, 1, -1)
@@ -211,6 +295,55 @@
     def last_z(dx):
         w_wait(dx, 2, EDGE_TOP)
         w_wait(dx, 2, EDGE_BOTTOM)
+
+    def unpack(dx, dz, which):
+        xx, zz = (x + dx + 4) % 4, (zh + dz + 4) % 4
+        block = w_row(dx, dz, which)
+        stage[:SLOTS] = packed[block]
+
+        @pl.loop(0, STRIPS)
+        def _(s):
+            t = (xx - s + 8) % 4
+            for source in range(4):
+                first = ((source * 4 + zz) * 2 + which) * ROWS + s * STRIP
+                for u in (0, 1):
+                    slot = table_smem[block, source * SHARE + 2 * s + u]
+                    piece = stage[jnp.clip(slot, 0, SLOTS)]
+                    weighted[t + 4 * u, pl.ds(pl.multiple_of(first, STRIP), STRIP)] = piece
+
+    pending = []
+
+    def ready(dx, dz):
+        share(dx, dz)
+        if sparse:
+            unpack(dx, dz, core)
+            pending.append((dx, dz))
+            if len(pending) > 2:
+                drain(1)
+
+    def drain(count):
+        for _ in range(count):
+            dx, dz = pending.pop(0)
+            shared(dx, dz)
+            unpack(dx, dz, 1 - core)
+
+    def multiply_pair(pair, first):
+        for n in range(0, COLS // TILE, 2):
+            width = min(2, COLS // TILE - n)
+            acc = None
+            for source in range(4):
+                group = source * 2 + pair
+                depth = pl.ds(pl.multiple_of(group * COLS, 16), COLS)
+                right = weighted[n, depth]
+                if width == 2:
+                    right = jnp.concatenate([right, weighted[n + 1, depth]], axis=1)
+                part = jnp.dot(panel[group], right, preferred_element_type=jnp.float32)
+                acc = part if acc is None else acc + part
+            columns = slice(n * TILE, (n + width) * TILE)
+            if first:
+                expanded[:, columns] = acc
+            else:
+                expanded[:, columns] += acc
 
     def multiply(dx, first):
         xx = (x + dx) % 4
@@ -231,6 +364,9 @@
             else:
                 expanded[:, start : start + size] += acc
 
+    if sparse:
+        unpack(0, 0, core)
+        pending.append((0, 0))
     w_wait(0, -1, TOP)
     w_send(0, -1, TOP, 1, 1)
     along_x(-1, TOP)
@@ -257,16 +393,16 @@
     w_wait(0, 1, TOP)
     along_x(1, TOP)
     rest_x(0)
-    share(-1, 0)
-    share(1, 0)
+    ready(-1, 0)
+    ready(1, 0)
     w_wait(2, 0, EDGE_TOP)
     w_wait(2, 0, EDGE_BOTTOM)
     along_z(2)
     last_x(0)
-    share(2, 0)
+    ready(2, 0)
     pass_z(0)
-    share(0, -1)
-    share(0, 1)
+    ready(0, -1)
+    ready(0, 1)
     w_wait(0, 2, TOP)
     along_x(2, TOP)
     w_wait(0, 2, BOTTOM)
@@ -276,100 +412,137 @@
     pass_x(1)
     pass_z(1)
     last_z(0)
-    share(0, 2)
+    ready(0, 2)
     a_wait(1, -1, 0)
     a_send_y(1, -1, 0, 1)
     a_wait(1, 1, 1)
     a_send_y(1, 1, 1, -1)
     rest_x(-1)
-    share(-1, -1)
-    share(1, -1)
+    ready(-1, -1)
+    ready(1, -1)
     rest_x(1)
-    share(-1, 1)
-    share(1, 1)
+    ready(-1, 1)
+    ready(1, 1)
     pass_z(2)
     last_x(-1)
-    share(2, -1)
+    ready(2, -1)
     last_x(1)
-    share(2, 1)
+    ready(2, 1)
     pass_x(2)
     for pair in (0, 1):
         for dy, half in ((-1, 1), (1, 0), (2, 0), (2, 1)):
             a_wait(pair, dy, half)
-    for dz in (0, -1, 1, 2):
-        shared(0, dz)
-    multiply(0, True)
+    if sparse:
+        drain(len(pending))
+        multiply_pair(zh // 2, True)
+    else:
+        for dz in (0, -1, 1, 2):
+            shared(0, dz)
+        multiply(0, True)
     rest_x(2)
     last_z(-1)
-    share(-1, 2)
+    ready(-1, 2)
     last_z(1)
-    share(1, 2)
+    ready(1, 2)
     last_z(2)
     last_x(2)
-    share(2, 2)
-    for dx in (-1, 1, 2):
-        for dz in (0, -1, 1, 2):
-            shared(dx, dz)
-        multiply(dx, False)
+    ready(2, 2)
+    if sparse:
+        drain(len(pending))
+        multiply_pair(1 - zh // 2, False)
+    else:
+        for dx in (-1, 1, 2):
+            for dz in (0, -1, 1, 2):
+                shared(dx, dz)
+            multiply(dx, False)
 
     inflated = expanded[...] * expanded[...]
-    part = jnp.sum(inflated.reshape(ROWS // 8, 8, COLS), axis=0)
-    total_own[0] = part
+    part = jnp.sum(inflated, axis=0, keepdims=True)
+    for t in range(COLS // TILE):
+        total_own[0, t : t + 1, :] = part[:, t * TILE : (t + 1) * TILE]
     send(total_own.at[0], total_core, recv_small.at[4], to_core)
     arrived(total_core, recv_small.at[4])
-    part += total_core[...]
-    total_own[1] = part
-    for d in (1, 3, 2):
+    total_own[1] = total_own[0] + total_core[...]
+    for d in (2, 1, 3):
         send(total_own.at[1], total_x.at[4 - d], recv_small.at[4 + 4 - d], to_x(d))
+    part = total_own[1]
     for d in (1, 3, 2):
         arrived(total_x.at[d], recv_small.at[4 + d])
         part += total_x[d]
     total_own[2] = part
-    for d in (1, 3, 2):
+    for d in (2, 1, 3):
         send(total_own.at[2], total_z.at[4 - d], recv_small.at[8 + 4 - d], to_z(d))
     for d in (1, 3, 2):
         arrived(total_z.at[d], recv_small.at[8 + d])
         part += total_z[d]
-    total = jnp.sum(part, axis=0, keepdims=True)
-    out_ref[...] = NODES * inflated / total
+    for t in range(COLS // TILE):
+        columns = slice(t * TILE, (t + 1) * TILE)
+        out_ref[:, columns] = NODES * inflated[:, columns] / part[t : t + 1, :]
     for copy in sends:
         copy.wait_send()
 
 
-def per_device(sim, live):
-    small = pltpu.VMEM((8, 256), jnp.float32)
-    wide = (8, COLS)
+def call(sparse, *operands):
+    vmem, sem = pltpu.VMEM, pltpu.SemaphoreType.DMA
+    bf16, f32, i32 = jnp.bfloat16, jnp.float32, jnp.int32
+    small, tile, table = (8, 256), (8, TILE), (32, TILE)
+    flow = jax.ShapeDtypeStruct((ROWS, COLS), f32)
+    in_vmem = pl.BlockSpec(memory_space=vmem)
+    extra = []
+    if sparse:
+        extra = [
+            vmem((ROW_DEVICES, SLOTS, STRIP, TILE), bf16),
+            vmem((4, SHARE, STRIP, TILE), bf16),
+            vmem((SPOTS, STRIP, TILE), bf16),
+            vmem((SLOTS + 1, STRIP, TILE), bf16),
+            vmem(table, f32),
+            vmem(table, f32),
+            vmem(table, i32),
+            pltpu.SMEM(table, i32),
+            vmem(table, i32),
+            pltpu.SMEM(table, i32),
+            sem((2,)),
+        ]
     return pl.pallas_call(
-        kernel,
-        out_shape=jax.ShapeDtypeStruct((ROWS, COLS), jnp.float32),
-        in_specs=[
-            pl.BlockSpec(memory_space=pltpu.VMEM),
-            pl.BlockSpec(memory_space=pltpu.SMEM),
-        ],
-        out_specs=pl.BlockSpec(memory_space=pltpu.VMEM),
+        functools.partial(kernel, sparse),
+        out_shape=[flow, jax.ShapeDtypeStruct(tile, f32)] if sparse else flow,
+        in_specs=[in_vmem, pl.BlockSpec(memory_space=pltpu.SMEM)] + [in_vmem] * (len(operands) - 2),
+        out_specs=[in_vmem, in_vmem] if sparse else in_vmem,
         scratch_shapes=[
-            pltpu.VMEM((COL_DEVICES, ROWS, COLS), jnp.bfloat16),
-            pltpu.VMEM((NODES, COLS), jnp.bfloat16),
-            pltpu.VMEM((ROWS, COLS), jnp.float32),
-            small,
-            small,
-            small,
-            pltpu.VMEM((4, 8, 256), jnp.float32),
-            pltpu.VMEM((3, *wide), jnp.float32),
-            pltpu.VMEM(wide, jnp.float32),
-            pltpu.VMEM((4, *wide), jnp.float32),
-            pltpu.VMEM((4, *wide), jnp.float32),
-            pltpu.SemaphoreType.DMA((SENDS,)),
-            pltpu.SemaphoreType.DMA((4, 4, 5)),
-            pltpu.SemaphoreType.DMA((4, 4)),
-            pltpu.SemaphoreType.DMA((2, 4, 2)),
-            pltpu.SemaphoreType.DMA((12,)),
+            *extra,
+            vmem((COL_DEVICES, ROWS, COLS), bf16),
+            vmem((8, NODES, TILE) if sparse else (NODES, COLS), bf16),
+            vmem((ROWS, COLS), f32),
+            vmem(small, f32),
+            vmem(small, f32),
+            vmem(small, f32),
+            vmem((4, *small), f32),
+            vmem((3, *tile), f32),
+            vmem(tile, f32),
+            vmem((4, *tile), f32),
+            vmem((4, *tile), f32),
+            sem((SENDS,)),
+            sem((4, 4, 5)),
+            sem((4, 4)),
+            sem((2, 4, 2)),
+            sem((12,)),
+            sem((4,)),
         ],
         compiler_params=pltpu.CompilerParams(
-            collective_id=0, has_side_effects=True, vmem_limit_bytes=56 * 2**20
+            collective_id=0 if sparse else 1,
+            has_side_effects=True,
+            vmem_limit_bytes=40 * 2**20,
         ),
-        name="expand_inflate",
-    )(sim, live)
+        name="flow_of_packed" if sparse else "flow_of_whole",
+    )(*operands)
+
+
+def per_device(sim, live):
+    marks = live.T
+    flow, most = call(True, sim, marks, marks, jnp.asarray(place_tables()))
+    return lax.cond(
+        most[0, TILE - 1] <= SLOTS, lambda: flow, lambda: call(False, sim, marks)
+    )
 
 
 def solution(mesh):

time: 94.5 us -> 76 us (0.80)
  Pallas kernels: 90.8 us -> 72.6 us
  local copies, waits for them, and re-layouts: 3.46 us -> 2.39 us
    pallas_call x1, Pallas kernels: 90.8 us -> 72.6 us  [call(): pl.pallas_call(functools.partial(kernel, sparse), out_shape=[flow, jax.Sh...]
    unnamed x2 -> x7, local copies, waits for them, and re-layouts: 3.46 us -> 1.81 us
where the time goes in v2:
time: 76 us; the launch traced here: 75.9 us
  Pallas kernels  72.6 us (96%)
  local copies, waits for them, and re-layouts  2.39 us (3%)
    pallas_call x1, Pallas kernels, call(): pl.pallas_call(functools.partial(kernel, sparse), out_shape=[flow, jax.Sh...  72.6 us
    unnamed x7, local copies, waits for them, and re-layouts  1.81 us

profile of v2, /device:TPU:32, one launch (start us, length us, event | category | flops | bytes accessed | tf_op | source)
XLA Modules:
  0.0 75.9 jit_solution(16125505493687191021)
XLA Ops:
  0.0 0.0 copy-start
  0.0 0.9 %copy-done = bf16[608,128]{1,0:T(8,128)(2,1)S(1)} copy-done((bf16[608,128]{1,0:T(8,128)(2,1)S(1)}, bf16[608,128]{1,0:T(8,128)(2,1)}, u32[]{:S(2)}) %copy-start) | copy-done | bytes 155672
  0.9 0.0 copy-start.1
  0.9 72.6 %flow_of_packed.1 = (f32[224,896]{1,0:T(8,128)S(1)}, f32[8,128]{1,0:T(8,128)S(1)}) custom-call(bf16[224,896]{1,0:T(8,128)(2,1)} %refs_0_.1, s32[7,56]{1,0:T(8,128)} %bitcast.2, s32[7,56]{1,0:T(8,128)} %bitcast.3, bf16[608,128]{1,0:T(8,128)(2,1)S(1)} %copy-done), custom_call_target="tpu_custom_call" | custom-call | tf_op jit(solution)/shard_map/flow_of_packed/pallas_call | solution.py:506
  73.5 0.0 copy-start.2
  73.5 0.6 slice.3
  74.7 0.0 copy-done.1
  74.8 0.0 copy-done.2
  74.8 0.2 conditional.1
  75.0 0.9 %copy.9 = f32[224,896]{1,0:T(8,128)} copy(f32[224,896]{1,0:T(8,128)S(1)} %get-tuple-element.19) | data formatting | bytes 1605632
Async XLA Ops:
  0.0 0.9 %copy-start = (bf16[608,128]{1,0:T(8,128)(2,1)S(1)}, bf16[608,128]{1,0:T(8,128)(2,1)}, u32[]{:S(2)}) copy-start(bf16[608,128]{1,0:T(8,128)(2,1)} %constant.5.clone.refs_3_) | copy-start | bytes 466948
  0.9 73.8 %copy-start.1 = (bf16[224,896]{1,0:T(8,128)(2,1)S(1)}, bf16[224,896]{1,0:T(8,128)(2,1)}, u32[]{:S(2)}) copy-start(bf16[224,896]{1,0:T(8,128)(2,1)} %refs_0_.1) | copy-start | bytes 1204228
  73.5 1.3 %copy-start.2 = (s32[56,7]{0,1:T(8,128)S(1)}, s32[56,7]{0,1:T(8,128)}, u32[]{:S(2)}) copy-start(s32[56,7]{0,1:T(8,128)} %param.6) | copy-start | bytes 4708

commit v3 on v2

--- a/solution.py
+++ b/solution.py
@@ -37,6 +37,26 @@
 SPOTS = 4 * SHARE
 PANEL_HALF = ROWS // 2
 SENDS = 112
+
+
+WEIGHTED, PANEL, SHARED, UNPACK, MULTIPLY = range(5)
+ORDER = (
+    (1, 1, 0, 0), (1, 0, 3, 0), (1, 0, 1, 1), (1, 1, 0, 1), (1, 0, 3, 1), (1, 0, 1, 0), (3, 0, 0, 0), (3, 0, 0, 1),
+    (0, 3, 0, 0), (0, 1, 0, 1), (0, 3, 0, 2), (0, 1, 0, 2), (0, 0, 3, 0), (0, 0, 1, 1), (0, 3, 0, 1), (2, 3, 0, 0),
+    (0, 1, 0, 0), (2, 1, 0, 0), (3, 3, 0, 0), (3, 1, 0, 0), (1, 1, 3, 0), (1, 0, 2, 1), (0, 2, 0, 0), (0, 2, 0, 1),
+    (0, 2, 0, 3), (0, 2, 0, 4), (2, 2, 0, 0), (3, 2, 0, 0), (3, 3, 0, 1), (3, 1, 0, 1), (0, 0, 3, 1), (0, 0, 1, 0),
+    (0, 3, 3, 0), (0, 1, 3, 0), (3, 2, 0, 1), (0, 3, 1, 1), (0, 1, 1, 1), (1, 0, 2, 0), (1, 1, 1, 1), (0, 0, 2, 0),
+    (0, 0, 2, 1), (0, 3, 3, 1), (0, 1, 3, 1), (0, 0, 3, 2), (2, 0, 3, 0), (0, 0, 1, 2), (2, 0, 1, 0), (3, 0, 3, 0),
+    (3, 0, 1, 0), (0, 3, 1, 0), (0, 1, 1, 0), (0, 3, 3, 2), (2, 3, 3, 0), (0, 3, 1, 2), (2, 3, 1, 0), (3, 3, 3, 0),
+    (3, 3, 1, 0), (3, 0, 3, 1), (1, 1, 2, 0), (0, 2, 3, 0), (0, 2, 1, 1), (0, 1, 3, 2), (2, 1, 3, 0), (1, 1, 1, 0),
+    (0, 1, 1, 2), (2, 1, 1, 0), (3, 0, 1, 1), (3, 1, 3, 0), (3, 1, 1, 0), (0, 2, 3, 3), (0, 2, 1, 3), (3, 3, 3, 1),
+    (3, 3, 1, 1), (0, 3, 2, 0), (0, 2, 3, 4), (0, 1, 2, 0), (0, 2, 1, 4), (0, 0, 2, 3), (0, 0, 2, 4), (2, 0, 2, 0),
+    (3, 1, 3, 1), (3, 0, 2, 0), (3, 1, 1, 1), (0, 3, 2, 3), (0, 3, 2, 4), (0, 3, 2, 1), (2, 3, 2, 0), (0, 1, 2, 1),
+    (3, 3, 2, 0), (0, 1, 2, 3), (0, 1, 2, 4), (2, 1, 2, 0), (3, 1, 2, 0), (1, 1, 3, 1), (0, 2, 2, 3), (1, 1, 2, 1),
+    (0, 2, 1, 0), (2, 2, 1, 0), (0, 2, 3, 1), (2, 2, 3, 0), (0, 2, 2, 4), (3, 0, 2, 1), (3, 2, 1, 0), (3, 2, 3, 0),
+    (3, 3, 2, 1), (3, 1, 2, 1), (0, 2, 2, 0), (0, 2, 2, 1), (2, 2, 2, 0), (3, 2, 1, 1), (3, 2, 3, 1), (4, 0, 0, 0),
+    (3, 2, 2, 0), (3, 2, 2, 1), (4, 1, 0, 0),
+)
 
 
 def place_tables():
@@ -60,7 +80,7 @@
 def kernel(sparse, *refs):
     if sparse:
         (sim_ref, live_ref, marks_ref, tables_ref, out_ref, flag_ref, *refs) = refs
-        (packed, out_share, in_share, stage, mark, order, table, table_smem, take, take_smem, copy_sem, *refs) = refs
+        (packed, out_share, in_share, stage, mark, order, table, table_smem, take, take_smem, copy_sem, degree_x, *refs) = refs
     else:
         sim_ref, live_ref, out_ref, *refs = refs
     (panel, weighted, expanded, degree_own, degree_pair, degree_sum, degree_in, total_own, total_core, total_x, total_z, *refs) = refs
@@ -137,6 +157,14 @@
         table_copy.start()
         take_copy.start()
         out_share[...] = jnp.zeros_like(out_share)
+        for q in range(4):
+            for s in range(STRIPS):
+                for u in (0, 1):
+                    t = (q - s) % 4 + 4 * u
+                    if t < COLS // TILE:
+                        out_share[q, s * 2 + u] = adj[
+                            s * STRIP : (s + 1) * STRIP, t * TILE : (t + 1) * TILE
+                        ]
         stage[SLOTS] = jnp.zeros((STRIP, TILE), jnp.bfloat16)
 
     pl.semaphore_wait(barrier, len(partners))
@@ -207,47 +235,53 @@
         arrived(w_block(dx, dz, 1 - core), recv_core.at[dx % 4, dz % 4])
 
     send(degree_own, degree_pair, recv_small.at[0], to_pair)
+    if sparse:
+        for d in (2, 1, 3):
+            there = (x + d) % 4
+            send(out_share.at[there], in_share.at[pl.ds(x * SHARE, SHARE)], recv_share.at[4 - d], to_x(d))
     for half in (0, 1):
         a_send_pair(half)
+    arrived(degree_pair, recv_small.at[0])
+    lane = lax.broadcasted_iota(jnp.int32, (8, 256), 1)
+
+    def join(a, b):
+        return jnp.where(lane < ROWS, a + b, jnp.maximum(a, b))
+
+    degree_sum[...] = join(degree_own[...], degree_pair[...])
+    for d in (1, 3, 2):
+        send(degree_sum, degree_in.at[4 - d], recv_small.at[4 - d], to_y(d))
     for half in (0, 1):
         a_send_y(0, 0, half, 1)
         a_send_y(0, 0, 1 - half, -1)
-    arrived(degree_pair, recv_small.at[0])
-    lane = lax.broadcasted_iota(jnp.int32, (8, 256), 1)
-
-    def join(a, b):
-        return jnp.where(lane < ROWS, a + b, jnp.maximum(a, b))
-
-    degree_sum[...] = join(degree_own[...], degree_pair[...])
-    for d in (1, 3, 2):
-        send(degree_sum, degree_in.at[4 - d], recv_small.at[4 - d], to_y(d))
     degree = degree_sum[...]
     for d in (1, 3, 2):
         arrived(degree_in.at[d], recv_small.at[d])
         degree = join(degree, degree_in[d])
-    degree_column = jnp.transpose(degree)[:ROWS, 0:1]
-    scaled = (adj.astype(jnp.float32) / degree_column).astype(jnp.bfloat16)
     if sparse:
         flag_ref[...] = degree[:, TILE:]
-        for q in range(4):
-            for s in range(STRIPS):
-                for u in (0, 1):
-                    t = (q - s) % 4 + 4 * u
-                    if t < COLS // TILE:
-                        out_share[q, s * 2 + u] = scaled[
-                            s * STRIP : (s + 1) * STRIP, t * TILE : (t + 1) * TILE
-                        ]
+        degree_x[0] = degree
         for d in (2, 1, 3):
-            there = (x + d) % 4
-            send(out_share.at[there], in_share.at[pl.ds(x * SHARE, SHARE)], recv_share.at[4 - d], to_x(d))
+            send(degree_x.at[0], degree_x.at[4 - d], recv_small.at[16 - d], to_x(d))
         in_share[pl.ds(x * SHARE, SHARE)] = out_share[x]
         table_copy.wait()
         take_copy.wait()
-        for d in (1, 3, 2):
-            arrived(in_share.at[pl.ds((x + d) % 4 * SHARE, SHARE)], recv_share.at[d])
+        for d in (0, 1, 3, 2):
+            source = (x + d) % 4
+            if d:
+                arrived(in_share.at[pl.ds(source * SHARE, SHARE)], recv_share.at[d])
+                arrived(degree_x.at[d], recv_small.at[12 + d])
+            degree_column = jnp.transpose(degree_x[d])[:ROWS, 0:1]
+            for s in range(STRIPS):
+                column = degree_column[s * STRIP : (s + 1) * STRIP]
+                for u in (0, 1):
+                    place = source * SHARE + 2 * s + u
+                    piece = in_share[place].astype(jnp.float32)
+                    in_share[place] = (piece / column).astype(jnp.bfloat16)
         for k in range(SLOTS):
             packed[row, k] = in_share[jnp.clip(take_smem[k, 0], 0, SPOTS - 1)]
     else:
+        degree_column = jnp.transpose(degree)[:ROWS, 0:1]
+        scaled = (adj.astype(jnp.float32) / degree_column).astype(jnp.bfloat16)
         weighted[pl.ds(pl.multiple_of(row * ROWS, 16), ROWS), :] = scaled
 
     w_send(0, 0, TOP, 1, 1)
@@ -260,41 +294,49 @@
     w_send(0, 0, TOP, 1, -1)
     w_send(0, 0, BOTTOM, 0, 1)
     w_send(0, 0, TOP, 0, -1)
-    w_send(0, 0, EDGE, 1, 1)
-    w_send(0, 0, EDGE, 1, -1)
     share(0, 0)
 
-    def along_x(dz, piece):
-        w_send(0, dz, piece, 0, 1)
-        w_send(0, dz, piece, 0, -1)
-
-    def along_z(dx):
-        w_send(dx, 0, EDGE, 1, 1)
-        w_send(dx, 0, EDGE, 1, -1)
-
-    def pass_x(dz):
-        w_wait(-1, dz, TOP)
-        w_send(-1, dz, TOP, 0, 1)
-        w_wait(1, dz, BOTTOM)
-        w_send(1, dz, BOTTOM, 0, -1)
-
-    def rest_x(dz):
-        w_wait(-1, dz, BOTTOM)
-        w_wait(1, dz, TOP)
-
-    def last_x(dz):
-        w_wait(2, dz, TOP)
-        w_wait(2, dz, BOTTOM)
-
-    def pass_z(dx):
-        w_wait(dx, -1, EDGE)
-        w_send(dx, -1, EDGE_TOP, 1, 1)
-        w_wait(dx, 1, EDGE)
-        w_send(dx, 1, EDGE_BOTTOM, 1, -1)
-
-    def last_z(dx):
-        w_wait(dx, 2, EDGE_TOP)
-        w_wait(dx, 2, EDGE_BOTTOM)
+    late = []
+
+    def edge_along_z(dx, piece):
+        if late is None:
+            w_send(dx, 0, piece, 1, 1)
+            w_send(dx, 0, piece, 1, -1)
+        else:
+            late.append((dx, piece))
+
+    def weighted_arrived(dx, dz, piece):
+        nonlocal late
+        w_wait(dx, dz, piece)
+        if dz == 0 and piece > BOTTOM:
+            if (dx, piece) in ((3, EDGE), (1, EDGE)):
+                w_send(dx, 0, EDGE_TOP if dx == 3 else EDGE_BOTTOM, 0, dx - 2)
+            edge_along_z(dx, piece)
+        elif piece > BOTTOM:
+            if dz == 3 and piece != EDGE_BOTTOM:
+                w_send(dx, dz, EDGE_TOP, 1, 1)
+            if dz == 1 and piece != EDGE_TOP:
+                w_send(dx, dz, EDGE_BOTTOM, 1, -1)
+        elif dx == 0:
+            if (dz, piece) in ((3, TOP), (1, BOTTOM)):
+                w_send(0, dz, piece, 1, dz - 2)
+            w_send(0, dz, piece, 0, 1)
+            w_send(0, dz, piece, 0, -1)
+        elif (dx, piece) in ((3, TOP), (1, BOTTOM)):
+            w_send(dx, dz, piece, 0, dx - 2)
+        if (dx, dz, piece) == (0, 3, BOTTOM):
+            held, late = late, None
+            for item in held:
+                edge_along_z(*item)
+
+    def panel_arrived(pair, dy, half):
+        a_wait(pair, dy, half)
+        if (pair, dy) == (1, 0):
+            a_send_y(1, 0, half, 1 - 2 * half)
+        if (pair, dy) == (0, 2):
+            a_send_y(1, 0, 1 - half, 1 - 2 * half)
+        if (dy, half) in ((3, 0), (1, 1)):
+            a_send_y(pair, dy, half, dy - 2)
 
     def unpack(dx, dz, which):
         xx, zz = (x + dx + 4) % 4, (zh + dz + 4) % 4
@@ -310,22 +352,6 @@
                     slot = table_smem[block, source * SHARE + 2 * s + u]
                     piece = stage[jnp.clip(slot, 0, SLOTS)]
                     weighted[t + 4 * u, pl.ds(pl.multiple_of(first, STRIP), STRIP)] = piece
-
-    pending = []
-
-    def ready(dx, dz):
-        share(dx, dz)
-        if sparse:
-            unpack(dx, dz, core)
-            pending.append((dx, dz))
-            if len(pending) > 2:
-                drain(1)
-
-    def drain(count):
-        for _ in range(count):
-            dx, dz = pending.pop(0)
-            shared(dx, dz)
-            unpack(dx, dz, 1 - core)
 
     def multiply_pair(pair, first):
         for n in range(0, COLS // TILE, 2):
@@ -364,97 +390,24 @@
             else:
                 expanded[:, start : start + size] += acc
 
-    if sparse:
-        unpack(0, 0, core)
-        pending.append((0, 0))
-    w_wait(0, -1, TOP)
-    w_send(0, -1, TOP, 1, 1)
-    along_x(-1, TOP)
-    w_wait(0, 1, BOTTOM)
-    w_send(0, 1, BOTTOM, 1, -1)
-    along_x(1, BOTTOM)
-    pass_x(0)
-    w_wait(-1, 0, EDGE)
-    w_send(-1, 0, EDGE_TOP, 0, 1)
-    along_z(-1)
-    w_wait(1, 0, EDGE)
-    w_send(1, 0, EDGE_BOTTOM, 0, -1)
-    along_z(1)
-    for half in (0, 1):
-        a_wait(1, 0, half)
-        a_send_y(1, 0, half, 1)
-        a_send_y(1, 0, half, -1)
-    a_wait(0, -1, 0)
-    a_send_y(0, -1, 0, 1)
-    a_wait(0, 1, 1)
-    a_send_y(0, 1, 1, -1)
-    w_wait(0, -1, BOTTOM)
-    along_x(-1, BOTTOM)
-    w_wait(0, 1, TOP)
-    along_x(1, TOP)
-    rest_x(0)
-    ready(-1, 0)
-    ready(1, 0)
-    w_wait(2, 0, EDGE_TOP)
-    w_wait(2, 0, EDGE_BOTTOM)
-    along_z(2)
-    last_x(0)
-    ready(2, 0)
-    pass_z(0)
-    ready(0, -1)
-    ready(0, 1)
-    w_wait(0, 2, TOP)
-    along_x(2, TOP)
-    w_wait(0, 2, BOTTOM)
-    along_x(2, BOTTOM)
-    pass_x(-1)
-    pass_z(-1)
-    pass_x(1)
-    pass_z(1)
-    last_z(0)
-    ready(0, 2)
-    a_wait(1, -1, 0)
-    a_send_y(1, -1, 0, 1)
-    a_wait(1, 1, 1)
-    a_send_y(1, 1, 1, -1)
-    rest_x(-1)
-    ready(-1, -1)
-    ready(1, -1)
-    rest_x(1)
-    ready(-1, 1)
-    ready(1, 1)
-    pass_z(2)
-    last_x(-1)
-    ready(2, -1)
-    last_x(1)
-    ready(2, 1)
-    pass_x(2)
-    for pair in (0, 1):
-        for dy, half in ((-1, 1), (1, 0), (2, 0), (2, 1)):
-            a_wait(pair, dy, half)
-    if sparse:
-        drain(len(pending))
-        multiply_pair(zh // 2, True)
-    else:
-        for dz in (0, -1, 1, 2):
-            shared(0, dz)
-        multiply(0, True)
-    rest_x(2)
-    last_z(-1)
-    ready(-1, 2)
-    last_z(1)
-    ready(1, 2)
-    last_z(2)
-    last_x(2)
-    ready(2, 2)
-    if sparse:
-        drain(len(pending))
-        multiply_pair(1 - zh // 2, False)
-    else:
-        for dx in (-1, 1, 2):
-            for dz in (0, -1, 1, 2):
-                shared(dx, dz)
-            multiply(dx, False)
+    edge_along_z(0, EDGE)
+    for act, first, second, third in ORDER:
+        if act == WEIGHTED:
+            weighted_arrived(first, second, third)
+        elif act == PANEL:
+            panel_arrived(first, second, third)
+        elif act == SHARED:
+            share(first, second)
+        elif act == UNPACK:
+            if third:
+                shared(first, second)
+            if sparse:
+                unpack(first, second, 1 - core if third else core)
+        elif sparse:
+            multiply_pair((zh // 2 + first) % 2, first == 0)
+    if not sparse:
+        for dx in range(4):
+            multiply(dx, dx == 0)
 
     inflated = expanded[...] * expanded[...]
     part = jnp.sum(inflated, axis=0, keepdims=True)
@@ -502,6 +455,7 @@
             vmem(table, i32),
             pltpu.SMEM(table, i32),
             sem((2,)),
+            vmem((4, *small), f32),
         ]
     return pl.pallas_call(
         functools.partial(kernel, sparse),
@@ -525,7 +479,7 @@
             sem((4, 4, 5)),
             sem((4, 4)),
             sem((2, 4, 2)),
-            sem((12,)),
+            sem((16,)),
             sem((4,)),
         ],
         compiler_params=pltpu.CompilerParams(

time: 76 us -> 65.4 us (0.86); the launches traced: 75.9 us -> 64.1 us
  Pallas kernels: 72.6 us -> 60.8 us
    pallas_call x1, Pallas kernels: 72.6 us -> 60.8 us  [call(): pl.pallas_call(functools.partial(kernel, sparse), out_shape=[flow, jax.Sh...]
where the time goes in v3:
time: 65.4 us; the launch traced here: 64.1 us
  Pallas kernels  60.8 us (93%)
  local copies, waits for them, and re-layouts  2.39 us (4%)
  between operations  0.7 us (1%)
    pallas_call x1, Pallas kernels, call(): pl.pallas_call(functools.partial(kernel, sparse), out_shape=[flow, jax.Sh...  60.8 us
    unnamed x7, local copies, waits for them, and re-layouts  1.81 us

profile of v3, /device:TPU:32, one launch (start us, length us, event | category | flops | bytes accessed | tf_op | source)
XLA Modules:
  0.0 64.1 jit_solution(17405059471246236418)
XLA Ops:
  0.0 0.0 copy-start
  0.0 0.9 %copy-done = bf16[608,128]{1,0:T(8,128)(2,1)S(1)} copy-done((bf16[608,128]{1,0:T(8,128)(2,1)S(1)}, bf16[608,128]{1,0:T(8,128)(2,1)}, u32[]{:S(2)}) %copy-start) | copy-done | bytes 155672
  0.9 0.0 copy-start.1
  0.9 60.8 %flow_of_packed.1 = (f32[224,896]{1,0:T(8,128)S(1)}, f32[8,128]{1,0:T(8,128)S(1)}) custom-call(bf16[224,896]{1,0:T(8,128)(2,1)} %refs_0_.1, s32[7,56]{1,0:T(8,128)} %bitcast.2, s32[7,56]{1,0:T(8,128)} %bitcast.3, bf16[608,128]{1,0:T(8,128)(2,1)S(1)} %copy-done), custom_call_target="tpu_custom_call" | custom-call | tf_op jit(solution)/shard_map/flow_of_packed/pallas_call | solution.py:460
  61.7 0.0 copy-start.2
  61.7 0.6 slice.3
  63.0 0.0 copy-done.1
  63.0 0.0 copy-done.2
  63.0 0.2 conditional.1
  63.2 0.9 %copy.9 = f32[224,896]{1,0:T(8,128)} copy(f32[224,896]{1,0:T(8,128)S(1)} %get-tuple-element.19) | data formatting | bytes 1605632
Async XLA Ops:
  0.0 0.9 %copy-start = (bf16[608,128]{1,0:T(8,128)(2,1)S(1)}, bf16[608,128]{1,0:T(8,128)(2,1)}, u32[]{:S(2)}) copy-start(bf16[608,128]{1,0:T(8,128)(2,1)} %constant.5.clone.refs_3_) | copy-start | bytes 466948
  0.9 62.1 %copy-start.1 = (bf16[224,896]{1,0:T(8,128)(2,1)S(1)}, bf16[224,896]{1,0:T(8,128)(2,1)}, u32[]{:S(2)}) copy-start(bf16[224,896]{1,0:T(8,128)(2,1)} %refs_0_.1) | copy-start | bytes 1204228
  61.7 1.3 %copy-start.2 = (s32[56,7]{0,1:T(8,128)S(1)}, s32[56,7]{0,1:T(8,128)}, u32[]{:S(2)}) copy-start(s32[56,7]{0,1:T(8,128)} %param.6) | copy-start | bytes 4708

commit v4 on v3

--- a/solution.py
+++ b/solution.py
@@ -36,7 +36,7 @@
 SHARE = 2 * STRIPS
 SPOTS = 4 * SHARE
 PANEL_HALF = ROWS // 2
-SENDS = 112
+SENDS = 128
 
 
 WEIGHTED, PANEL, SHARED, UNPACK, MULTIPLY = range(5)
@@ -83,7 +83,7 @@
         (packed, out_share, in_share, stage, mark, order, table, table_smem, take, take_smem, copy_sem, degree_x, *refs) = refs
     else:
         sim_ref, live_ref, out_ref, *refs = refs
-    (panel, weighted, expanded, degree_own, degree_pair, degree_sum, degree_in, total_own, total_core, total_x, total_z, *refs) = refs
+    (panel, weighted, expanded, degree_own, degree_in, total_own, total_core, total_x, total_z, *refs) = refs
     send_sem, recv_w, recv_core, recv_a, recv_small, recv_share = refs
     row, col = lax.axis_index("row"), lax.axis_index("col")
     x, zh, core = row // 8, (row // 2) % 4, row % 2
@@ -101,8 +101,12 @@
     to_pair = (row, (1 - zl) * 4 + y)
     to_core = (row + 1 - 2 * core, col)
 
+    def to_pair_y(d):
+        return row, (1 - zl) * 4 + (y + d + 4) % 4
+
+
     barrier = pltpu.get_barrier_semaphore()
-    partners = [to(d) for to in (to_x, to_y, to_z) for d in (1, 2, 3)] + [to_pair, to_core]
+    partners = [to(d) for to in (to_x, to_y, to_z, to_pair_y) for d in (1, 2, 3)] + [to_pair, to_core]
     for device in partners:
         pl.semaphore_signal(barrier, 1, device_id=device, device_id_type=MESH)
 
@@ -234,28 +238,29 @@
     def shared(dx, dz):
         arrived(w_block(dx, dz, 1 - core), recv_core.at[dx % 4, dz % 4])
 
-    send(degree_own, degree_pair, recv_small.at[0], to_pair)
+    for d in (2, 1, 3):
+        send(degree_own, degree_in.at[8 - d], recv_small.at[24 - d], to_pair_y(d))
+    for d in (2, 1, 3):
+        send(degree_own, degree_in.at[4 - d], recv_small.at[20 - d], to_y(d))
+    send(degree_own, degree_in.at[4], recv_small.at[20], to_pair)
     if sparse:
         for d in (2, 1, 3):
             there = (x + d) % 4
             send(out_share.at[there], in_share.at[pl.ds(x * SHARE, SHARE)], recv_share.at[4 - d], to_x(d))
     for half in (0, 1):
         a_send_pair(half)
-    arrived(degree_pair, recv_small.at[0])
-    lane = lax.broadcasted_iota(jnp.int32, (8, 256), 1)
-
-    def join(a, b):
-        return jnp.where(lane < ROWS, a + b, jnp.maximum(a, b))
-
-    degree_sum[...] = join(degree_own[...], degree_pair[...])
-    for d in (1, 3, 2):
-        send(degree_sum, degree_in.at[4 - d], recv_small.at[4 - d], to_y(d))
     for half in (0, 1):
         a_send_y(0, 0, half, 1)
         a_send_y(0, 0, 1 - half, -1)
-    degree = degree_sum[...]
-    for d in (1, 3, 2):
-        arrived(degree_in.at[d], recv_small.at[d])
+
+    lane = lax.broadcasted_iota(jnp.int32, (8, 256), 1)
+
+    def join(a, b):
+        return jnp.where(lane < ROWS, a + b, jnp.maximum(a, b))
+
+    degree = degree_own[...]
+    for d in (4, 1, 3, 2, 5, 7, 6):
+        arrived(degree_in.at[d], recv_small.at[16 + d])
         degree = join(degree, degree_in[d])
     if sparse:
         flag_ref[...] = degree[:, TILE:]
@@ -356,15 +361,20 @@
     def multiply_pair(pair, first):
         for n in range(0, COLS // TILE, 2):
             width = min(2, COLS // TILE - n)
-            acc = None
+            left, right = [], []
             for source in range(4):
                 group = source * 2 + pair
                 depth = pl.ds(pl.multiple_of(group * COLS, 16), COLS)
-                right = weighted[n, depth]
+                part = weighted[n, depth]
                 if width == 2:
-                    right = jnp.concatenate([right, weighted[n + 1, depth]], axis=1)
-                part = jnp.dot(panel[group], right, preferred_element_type=jnp.float32)
-                acc = part if acc is None else acc + part
+                    part = jnp.concatenate([part, weighted[n + 1, depth]], axis=1)
+                left.append(panel[group])
+                right.append(part)
+            acc = jnp.dot(
+                jnp.concatenate(left, axis=1),
+                jnp.concatenate(right, axis=0),
+                preferred_element_type=jnp.float32,
+            )
             columns = slice(n * TILE, (n + width) * TILE)
             if first:
                 expanded[:, columns] = acc
@@ -468,9 +478,7 @@
             vmem((8, NODES, TILE) if sparse else (NODES, COLS), bf16),
             vmem((ROWS, COLS), f32),
             vmem(small, f32),
-            vmem(small, f32),
-            vmem(small, f32),
-            vmem((4, *small), f32),
+            vmem((8, *small), f32),
             vmem((3, *tile), f32),
             vmem(tile, f32),
             vmem((4, *tile), f32),
@@ -479,7 +487,7 @@
             sem((4, 4, 5)),
             sem((4, 4)),
             sem((2, 4, 2)),
-            sem((16,)),
+            sem((32,)),
             sem((4,)),
         ],
         compiler_params=pltpu.CompilerParams(

time: 65.4 us -> 64.9 us (level)
  no operation moved by 1% of the time
where the time goes in v4:
time: 64.9 us; the launch traced here: 64 us
  Pallas kernels  60.7 us (94%)
  local copies, waits for them, and re-layouts  2.39 us (4%)
  between operations  0.7 us (1%)
    pallas_call x1, Pallas kernels, call(): pl.pallas_call(functools.partial(kernel, sparse), out_shape=[flow, jax.Sh...  60.7 us
    unnamed x7, local copies, waits for them, and re-layouts  1.81 us

profile of v4, /device:TPU:32, one launch (start us, length us, event | category | flops | bytes accessed | tf_op | source)
XLA Modules:
  0.0 64.0 jit_solution(1543062344605208132)
XLA Ops:
  0.0 0.0 copy-start
  0.0 0.9 %copy-done = bf16[608,128]{1,0:T(8,128)(2,1)S(1)} copy-done((bf16[608,128]{1,0:T(8,128)(2,1)S(1)}, bf16[608,128]{1,0:T(8,128)(2,1)}, u32[]{:S(2)}) %copy-start) | copy-done | bytes 155672
  0.9 0.0 copy-start.1
  0.9 60.7 %flow_of_packed.1 = (f32[224,896]{1,0:T(8,128)S(1)}, f32[8,128]{1,0:T(8,128)S(1)}) custom-call(bf16[224,896]{1,0:T(8,128)(2,1)} %refs_0_.1, s32[7,56]{1,0:T(8,128)} %bitcast.2, s32[7,56]{1,0:T(8,128)} %bitcast.3, bf16[608,128]{1,0:T(8,128)(2,1)S(1)} %copy-done), custom_call_target="tpu_custom_call" | custom-call | tf_op jit(solution)/shard_map/flow_of_packed/pallas_call | solution.py:470
  61.6 0.0 copy-start.2
  61.6 0.6 slice.3
  62.9 0.0 copy-done.1
  62.9 0.0 copy-done.2
  62.9 0.2 conditional.1
  63.1 0.9 %copy.9 = f32[224,896]{1,0:T(8,128)} copy(f32[224,896]{1,0:T(8,128)S(1)} %get-tuple-element.19) | data formatting | bytes 1605632
Async XLA Ops:
  0.0 0.9 %copy-start = (bf16[608,128]{1,0:T(8,128)(2,1)S(1)}, bf16[608,128]{1,0:T(8,128)(2,1)}, u32[]{:S(2)}) copy-start(bf16[608,128]{1,0:T(8,128)(2,1)} %constant.5.clone.refs_3_) | copy-start | bytes 466948
  0.9 62.0 %copy-start.1 = (bf16[224,896]{1,0:T(8,128)(2,1)S(1)}, bf16[224,896]{1,0:T(8,128)(2,1)}, u32[]{:S(2)}) copy-start(bf16[224,896]{1,0:T(8,128)(2,1)} %refs_0_.1) | copy-start | bytes 1204228
  61.6 1.3 %copy-start.2 = (s32[56,7]{0,1:T(8,128)S(1)}, s32[56,7]{0,1:T(8,128)}, u32[]{:S(2)}) copy-start(s32[56,7]{0,1:T(8,128)} %param.6) | copy-start | bytes 4708

commit v5 on v4

--- a/solution.py
+++ b/solution.py
@@ -80,7 +80,7 @@
 def kernel(sparse, *refs):
     if sparse:
         (sim_ref, live_ref, marks_ref, tables_ref, out_ref, flag_ref, *refs) = refs
-        (packed, out_share, in_share, stage, mark, order, table, table_smem, take, take_smem, copy_sem, degree_x, *refs) = refs
+        (packed, out_share, in_share, stage, mark, order, table, table_smem, take, take_smem, copy_sem, degree_x, degree_strip, *refs) = refs
     else:
         sim_ref, live_ref, out_ref, *refs = refs
     (panel, weighted, expanded, degree_own, degree_in, total_own, total_core, total_x, total_z, *refs) = refs
@@ -270,20 +270,23 @@
         in_share[pl.ds(x * SHARE, SHARE)] = out_share[x]
         table_copy.wait()
         take_copy.wait()
-        for d in (0, 1, 3, 2):
-            source = (x + d) % 4
-            if d:
-                arrived(in_share.at[pl.ds(source * SHARE, SHARE)], recv_share.at[d])
-                arrived(degree_x.at[d], recv_small.at[12 + d])
-            degree_column = jnp.transpose(degree_x[d])[:ROWS, 0:1]
+        for d in (1, 3, 2):
+            arrived(degree_x.at[d], recv_small.at[12 + d])
+        ring = lax.broadcasted_iota(jnp.int32, (8, 256), 0)
+        columns = degree
+        for d in (1, 2, 3):
+            columns = jnp.where(ring == d, degree_x[d], columns)
+        columns = jnp.transpose(columns)
+        for d in range(4):
             for s in range(STRIPS):
-                column = degree_column[s * STRIP : (s + 1) * STRIP]
-                for u in (0, 1):
-                    place = source * SHARE + 2 * s + u
-                    piece = in_share[place].astype(jnp.float32)
-                    in_share[place] = (piece / column).astype(jnp.bfloat16)
+                column = columns[s * STRIP : (s + 1) * STRIP, d : d + 1]
+                degree_strip[(x + d) % 4 * STRIPS + s] = jnp.broadcast_to(column, (STRIP, TILE))
+        for d in (1, 3, 2):
+            arrived(in_share.at[pl.ds((x + d) % 4 * SHARE, SHARE)], recv_share.at[d])
         for k in range(SLOTS):
-            packed[row, k] = in_share[jnp.clip(take_smem[k, 0], 0, SPOTS - 1)]
+            place = jnp.clip(take_smem[k, 0], 0, SPOTS - 1)
+            piece = in_share[place].astype(jnp.float32) / degree_strip[place // 2]
+            packed[row, k] = piece.astype(jnp.bfloat16)
     else:
         degree_column = jnp.transpose(degree)[:ROWS, 0:1]
         scaled = (adj.astype(jnp.float32) / degree_column).astype(jnp.bfloat16)
@@ -379,7 +382,8 @@
             if first:
                 expanded[:, columns] = acc
             else:
-                expanded[:, columns] += acc
+                acc += expanded[:, columns]
+                expanded[:, columns] = acc * acc
 
     def multiply(dx, first):
         xx = (x + dx) % 4
@@ -419,7 +423,7 @@
         for dx in range(4):
             multiply(dx, dx == 0)
 
-    inflated = expanded[...] * expanded[...]
+    inflated = expanded[...] if sparse else expanded[...] * expanded[...]
     part = jnp.sum(inflated, axis=0, keepdims=True)
     for t in range(COLS // TILE):
         total_own[0, t : t + 1, :] = part[:, t * TILE : (t + 1) * TILE]
@@ -466,6 +470,7 @@
             pltpu.SMEM(table, i32),
             sem((2,)),
             vmem((4, *small), f32),
+            vmem((4 * STRIPS, STRIP, TILE), f32),
         ]
     return pl.pallas_call(
         functools.partial(kernel, sparse),

time: 64.9 us -> 64.9 us (level)
  no operation moved by 1% of the time
where the time goes in v5:
time: 64.9 us; the launch traced here: 64 us
  Pallas kernels  60.7 us (94%)
  local copies, waits for them, and re-layouts  2.39 us (4%)
  between operations  0.7 us (1%)
    pallas_call x1, Pallas kernels, call(): pl.pallas_call(functools.partial(kernel, sparse), out_shape=[flow, jax.Sh...  60.7 us
    unnamed x7, local copies, waits for them, and re-layouts  1.81 us

profile of v5, /device:TPU:32, one launch (start us, length us, event | category | flops | bytes accessed | tf_op | source)
XLA Modules:
  0.0 64.0 jit_solution(266650371458520724)
XLA Ops:
  0.0 0.0 copy-start
  0.0 0.9 %copy-done = bf16[608,128]{1,0:T(8,128)(2,1)S(1)} copy-done((bf16[608,128]{1,0:T(8,128)(2,1)S(1)}, bf16[608,128]{1,0:T(8,128)(2,1)}, u32[]{:S(2)}) %copy-start) | copy-done | bytes 155672
  0.9 0.0 copy-start.1
  0.9 60.7 %flow_of_packed.1 = (f32[224,896]{1,0:T(8,128)S(1)}, f32[8,128]{1,0:T(8,128)S(1)}) custom-call(bf16[224,896]{1,0:T(8,128)(2,1)} %refs_0_.1, s32[7,56]{1,0:T(8,128)} %bitcast.2, s32[7,56]{1,0:T(8,128)} %bitcast.3, bf16[608,128]{1,0:T(8,128)(2,1)S(1)} %copy-done), custom_call_target="tpu_custom_call" | custom-call | tf_op jit(solution)/shard_map/flow_of_packed/pallas_call | solution.py:475
  61.6 0.0 copy-start.2
  61.7 0.6 slice.3
  62.9 0.0 copy-done.1
  62.9 0.0 copy-done.2
  62.9 0.2 conditional.1
  63.1 0.9 %copy.9 = f32[224,896]{1,0:T(8,128)} copy(f32[224,896]{1,0:T(8,128)S(1)} %get-tuple-element.19) | data formatting | bytes 1605632
Async XLA Ops:
  0.0 0.9 %copy-start = (bf16[608,128]{1,0:T(8,128)(2,1)S(1)}, bf16[608,128]{1,0:T(8,128)(2,1)}, u32[]{:S(2)}) copy-start(bf16[608,128]{1,0:T(8,128)(2,1)} %constant.5.clone.refs_3_) | copy-start | bytes 466948
  0.9 62.0 %copy-start.1 = (bf16[224,896]{1,0:T(8,128)(2,1)S(1)}, bf16[224,896]{1,0:T(8,128)(2,1)}, u32[]{:S(2)}) copy-start(bf16[224,896]{1,0:T(8,128)(2,1)} %refs_0_.1) | copy-start | bytes 1204228
  61.6 1.3 %copy-start.2 = (s32[56,7]{0,1:T(8,128)S(1)}, s32[56,7]{0,1:T(8,128)}, u32[]{:S(2)}) copy-start(s32[56,7]{0,1:T(8,128)} %param.6) | copy-start | bytes 4708
